TPU v7x, 32 devices: a whole 2x2x4 slice. The times are simulated.
32 devices in a mesh: blk: 4 (over y, x), tile: 8 (over z, core).
Axes of the slice: x: 2, y: 2, z: 4, core: 2. Of those that a mesh axis runs over, the one named last changes fastest.
Arguments:
- grid_feat: bfloat16 [8192, 512], P(('blk', 'tile')), may hold values from -18 to 18
- queries: bfloat16 [8192, 512], P(('blk', 'tile')), may hold values from -90 to 90
- obs_keys: bfloat16 [256, 512], P(('blk', 'tile')), may hold values from -4 to 4
- obs_values: bfloat16 [256, 512], P(('blk', 'tile')), may hold values from -6 to 6
- block_mask: int32 [64, 2], P(('blk', 'tile')), may hold values from 0 to 1, as said below
- obs_valid: int32 [2], replicated, may hold values from 2 to 128, as said below
- out_weight: bfloat16 [512, 512], replicated, may hold values from -0.25 to 0.25
- conv_weight: bfloat16 [3, 3, 512, 512], replicated, may hold values from -0.09375 to 0.09375
Outputs:
- layer_out: bfloat16 [8192, 512], P(('blk', 'tile'))
Inputs may be any that keep to these rules, and one draw needn't show every extreme that they name: `block_mask`: row t has a 1 in column t mod 2. `obs_valid`: at least one entry equals 128.
All inputs are finite; a program needn't handle non-finite values.
Results may differ from a plain program's by a relative error of at most 0.007.
Values may be sent and summed in bfloat16 or wider, within the bound.
No kernel may reach another device: no remote copies, remote signals or barrier semaphores. Data moves between devices by JAX's collectives and lax.ppermute only.
A program may use at most 64 MiB of HBM per device.

v0:
```python
import jax
import jax.numpy as jnp
from jax import lax
from jax.sharding import PartitionSpec as P

HEADS = 8
OBS_BLOCK = 128


def passed_along(array, axis, by):
    peers = lax.axis_size(axis)
    return lax.ppermute(array, axis, [(i, (i + by) % peers) for i in range(peers)])


def with_halo(block, sides, width):
    for axis, dim in sides:
        count = lax.axis_size(axis)
        forward = [(i, i + 1) for i in range(count - 1)]
        backward = [(target, source) for source, target in forward]
        low = lax.ppermute(
            lax.slice_in_dim(block, block.shape[dim] - width, None, axis=dim), axis, forward
        )
        high = lax.ppermute(lax.slice_in_dim(block, 0, width, axis=dim), axis, backward)
        block = jnp.concatenate([low, block, high], axis=dim)
    return block


def circulate(block, visit, carry):
    home = lax.axis_index("blk")
    count = lax.axis_size("blk")
    carry = visit(carry, block, home)
    for step in range(1, count):
        block = passed_along(block, "blk", 1)
        carry = visit(carry, block, (home - step) % count)
    return carry


def on_device(
    grid_feat, queries, obs_keys, obs_values, block_mask, obs_valid, out_weight, conv_weight
):
    q_dev, width = queries.shape
    head = width // HEADS
    scale = head ** (-0.5)
    tiles = block_mask.shape[0]
    nblocks = block_mask.shape[1]
    lon = q_dev // tiles
    group_rows = obs_keys.shape[0] * lax.axis_size("tile")
    query_heads = queries.reshape(q_dev, HEADS, head)
    mask_float = block_mask.astype(jnp.float32)
    block_ids = jnp.arange(nblocks, dtype=jnp.int32)

    def attend(carry, kv_rows, start):
        rows = kv_rows.shape[1]
        key_index = start + jnp.arange(rows, dtype=jnp.int32)
        member = (key_index // OBS_BLOCK)[:, None] == block_ids[None, :]
        limits = jnp.sum(jnp.where(member, obs_valid[None, :], 0), axis=1)
        live = key_index % OBS_BLOCK < limits
        wanted = (
            jnp.dot(mask_float, member.astype(jnp.float32).T, precision=lax.Precision.HIGHEST) > 0.5
        )
        allowed = wanted & live[None, :]
        top, total, acc = carry
        keys = kv_rows[0].reshape(rows, HEADS, head)
        values = kv_rows[1].reshape(rows, HEADS, head)
        scores = (
            jnp.einsum("qhd,khd->hqk", query_heads, keys, preferred_element_type=jnp.float32)
            * scale
        )
        scores = scores.reshape(HEADS, tiles, lon, rows)
        scores = jnp.where(allowed[None, :, None, :], scores, -jnp.inf).reshape(HEADS, q_dev, rows)
        new_top = jnp.maximum(top, jnp.max(scores, axis=-1))
        factor = jnp.exp(top - new_top)
        weights = jnp.exp(scores - new_top[..., None])
        total = total * factor + jnp.sum(weights, axis=-1)
        acc = acc * factor[..., None] + jnp.einsum(
            "hqk,khd->hqd", weights.astype(jnp.bfloat16), values, preferred_element_type=jnp.float32
        )
        return (new_top, total, acc)

    start_state = (
        jnp.full((HEADS, q_dev), -1e30, jnp.float32),
        jnp.zeros((HEADS, q_dev), jnp.float32),
        jnp.zeros((HEADS, q_dev, head), jnp.float32),
    )
    kv_local = jnp.stack([obs_keys, obs_values])

    def visit_shards(carry, block, owner):
        collected = lax.all_gather(block, "tile", axis=1, tiled=True)
        return attend(carry, collected, owner * group_rows)

    state = circulate(kv_local, visit_shards, start_state)
    top, total, acc = state
    mixed = (
        jnp.transpose(acc / total[..., None], (1, 0, 2)).reshape(q_dev, width).astype(jnp.bfloat16)
    )
    projected = jnp.dot(mixed, out_weight, preferred_element_type=jnp.float32)
    hidden = lax.optimization_barrier(
        (grid_feat.astype(jnp.float32) + projected).astype(jnp.bfloat16)
    )
    wide = hidden.astype(jnp.float32)
    normed = (wide * lax.rsqrt(jnp.mean(wide * wide, axis=-1, keepdims=True) + 1e-06)).astype(
        jnp.bfloat16
    )
    field = normed.reshape(tiles, lon, width)
    padded = with_halo(field, ((("blk", "tile"), 0),), 1)
    summed = jnp.zeros((q_dev, width), jnp.float32)
    for lat_off in range(3):
        for lon_off in range(3):
            moved = jnp.roll(padded[lat_off : lat_off + tiles], 1 - lon_off, axis=1)
            summed = summed + jnp.dot(
                moved.reshape(q_dev, width),
                conv_weight[lat_off, lon_off],
                preferred_element_type=jnp.float32,
            )
    return (wide + summed).astype(jnp.bfloat16)


def solution(mesh):
    in_specs = (
        P(("blk", "tile"), None),
        P(("blk", "tile"), None),
        P(("blk", "tile"), None),
        P(("blk", "tile"), None),
        P(("blk", "tile"), None),
        P(),
        P(),
        P(),
    )
    out_specs = P(("blk", "tile"), None)
    return jax.shard_map(
        on_device, mesh=mesh, in_specs=in_specs, out_specs=out_specs, check_vma=False
    )
```

profile of v0, /device:TPU:4, one launch (start us, length us, event | category | flops | bytes accessed | tf_op | source)
XLA Modules:
  0.0 95.7 jit_solution(1427479328024810203)
XLA Ops:
  0.0 0.8 pad_maximum_fusion.6
  0.8 1.5 %collective-permute-start = (bf16[2,8,512]{2,1,0:T(8,128)(2,1)S(1)}, bf16[2,8,512]{2,1,0:T(8,128)(2,1)S(1)}, u32[]{:S(2)}, u32[]{:S(2)}) collective-permute-start(bf16[2,8,512]{2,1,0:T(8,128)(2,1)S(1)} %pad_maximum_fusion.6), channel_id=1, source_target_pairs={{0,8},{8,16},{16,24},{24,0},{1,9},{9,17},{17,25},{25,1},{2,10},{10... | collective-permute-start | bytes 49160 | tf_op jit(solution)/shard_map/ppermute | solution.py:12
  2.3 14.2 %all_gather.12 = bf16[2,64,512]{2,1,0:T(8,128)(2,1)S(1)} all-gather(bf16[2,8,512]{2,1,0:T(8,128)(2,1)S(1)} %pad_maximum_fusion.6), channel_id=1, replica_groups=mesh['blk'=4,'tile'=8] {'tile'}, dimensions={1}, use_global_device_ids=true | all-gather | bytes 147456 | tf_op jit(solution)/shard_map/all_gather | solution.py:88
  16.6 0.7 select_reduce_fusion
  17.3 0.8 fusion.25
  18.1 0.8 fusion.27
  19.0 0.8 fusion.21
  20.2 1.1 %copy.35 = bf16[256,512]{0,1:T(8,128)(2,1)S(1)} copy(bf16[256,512]{1,0:T(8,128)(2,1)} %param.9) | data formatting | bytes 524288 | tf_op args[1]
  21.5 0.8 fusion.23
  23.3 14.0 %all_gather.13 = bf16[2,64,512]{2,1,0:T(8,128)(2,1)S(1)} all-gather(bf16[2,8,512]{2,1,0:T(8,128)(2,1)S(1)} %collective-permute-done), channel_id=1, replica_groups=mesh['blk'=4,'tile'=8] {'tile'}, dimensions={1}, use_global_device_ids=true | all-gather | bytes 147456 | tf_op jit(solution)/shard_map/all_gather | solution.py:88
  37.4 0.5 collective-permute-start.1
  38.3 3.8 %collective-permute-done.1 = bf16[2,8,512]{2,1,0:T(8,128)(2,1)S(1)} collective-permute-done((bf16[2,8,512]{2,1,0:T(8,128)(2,1)S(1)}, bf16[2,8,512]{2,1,0:T(8,128)(2,1)S(1)}, u32[]{:S(2)}, u32[]{:S(2)}) %collective-permute-start.1) | collective-permute-done | bytes 16416 | tf_op jit(solution)/shard_map/ppermute | solution.py:12
  42.1 14.0 %all_gather.14 = bf16[2,64,512]{2,1,0:T(8,128)(2,1)S(1)} all-gather(bf16[2,8,512]{2,1,0:T(8,128)(2,1)S(1)} %collective-permute-done.1), channel_id=1, replica_groups=mesh['blk'=4,'tile'=8] {'tile'}, dimensions={1}, use_global_device_ids=true | all-gather | bytes 147456 | tf_op jit(solution)/shard_map/all_gather | solution.py:88
  56.7 4.3 %collective-permute-done.2 = bf16[2,8,512]{2,1,0:T(8,128)(2,1)S(1)} collective-permute-done((bf16[2,8,512]{2,1,0:T(8,128)(2,1)S(1)}, bf16[2,8,512]{2,1,0:T(8,128)(2,1)S(1)}, u32[]{:S(2)}, u32[]{:S(2)}) %collective-permute-start.2) | collective-permute-done | bytes 16416 | tf_op jit(solution)/shard_map/ppermute | solution.py:12
  61.0 14.0 %all_gather.15 = bf16[2,64,512]{2,1,0:T(8,128)(2,1)S(1)} all-gather(bf16[2,8,512]{2,1,0:T(8,128)(2,1)S(1)} %collective-permute-done.2), channel_id=1, replica_groups=mesh['blk'=4,'tile'=8] {'tile'}, dimensions={1}, use_global_device_ids=true | all-gather | bytes 147456 | tf_op jit(solution)/shard_map/all_gather | solution.py:88
  77.0 0.3 fusion.18
  77.6 4.3 %collective-permute-start.4 = (bf16[1,128,512]{2,1,0:T(8,128)(2,1)S(1)}, bf16[1,128,512]{2,1,0:T(8,128)(2,1)S(1)}, u32[]{:S(2)}, u32[]{:S(2)}) collective-permute-start(bf16[1,128,512]{2,1,0:T(8,128)(2,1)S(1)} %get-tuple-element.32), channel_id=1, source_target_pairs={{1,0},{2,1},{3,2},{4,3},{5,4},{6,5},{7,6},{8,7},{9,8},{10,9},{11,1... | collective-permute-start | bytes 393224 | tf_op jit(solution)/shard_map/ppermute | solution.py:23
  81.8 1.9 %collective-permute-start.3 = (bf16[1,128,512]{2,1,0:T(8,128)(2,1)S(1)}, bf16[1,128,512]{2,1,0:T(8,128)(2,1)S(1)}, u32[]{:S(2)}, u32[]{:S(2)}) collective-permute-start(bf16[1,128,512]{2,1,0:T(8,128)(2,1)S(1)} %get-tuple-element.33), channel_id=1, source_target_pairs={{0,1},{1,2},{2,3},{3,4},{4,5},{5,6},{6,7},{7,8},{8,9},{9,10},{10,1... | collective-permute-start | bytes 393224 | tf_op jit(solution)/shard_map/ppermute | solution.py:20
  83.8 1.0 %collective-permute-done.4 = bf16[1,128,512]{2,1,0:T(8,128)(2,1)S(1)} collective-permute-done((bf16[1,128,512]{2,1,0:T(8,128)(2,1)S(1)}, bf16[1,128,512]{2,1,0:T(8,128)(2,1)S(1)}, u32[]{:S(2)}, u32[]{:S(2)}) %collective-permute-start.4) | collective-permute-done | bytes 131104 | tf_op jit(solution)/shard_map/ppermute | solution.py:23
  84.8 7.0 %collective-permute-done.3 = bf16[1,128,512]{2,1,0:T(8,128)(2,1)S(1)} collective-permute-done((bf16[1,128,512]{2,1,0:T(8,128)(2,1)S(1)}, bf16[1,128,512]{2,1,0:T(8,128)(2,1)S(1)}, u32[]{:S(2)}, u32[]{:S(2)}) %collective-permute-start.3) | collective-permute-done | bytes 131104 | tf_op jit(solution)/shard_map/ppermute | solution.py:20
  92.6 0.3 convolution_add_fusion.7
  93.2 0.3 convolution_add_fusion.5
  93.8 0.3 convolution_add_fusion.3
  94.7 1.0 %fusion.17 = bf16[256,512]{1,0:T(8,128)(2,1)} fusion(f32[256,512]{1,0:T(8,128)S(1)} %convolution_add_fusion.1, bf16[256,512]{1,0:T(8,128)(2,1)S(1)} %bitcast.215, bf16[256,512]{1,0:T(8,128)(2,1)S(1)} %fusion.18, bf16[3,3,512,512]{3,2,1,0:T(8,128)(2,1)S(1)} %bitcast.214), kind=kOutput, calls=%fused_computation.34 | convolution fusion | flops 134742016 | bytes 1835008 | tf_op jit(solution)/shard_map/dot_general | solution.py:110
  (69 shorter events, 6.7 us)
Async XLA Ops:
  0.0 76.9 %copy-start = (bf16[512,512]{1,0:T(8,128)(2,1)S(1)}, bf16[512,512]{1,0:T(8,128)(2,1)}, u32[]{:S(2)}) copy-start(bf16[512,512]{1,0:T(8,128)(2,1)} %param.14) | copy-start | bytes 1572868
  0.8 22.5 %collective-permute-start = (bf16[2,8,512]{2,1,0:T(8,128)(2,1)S(1)}, bf16[2,8,512]{2,1,0:T(8,128)(2,1)S(1)}, u32[]{:S(2)}, u32[]{:S(2)}) collective-permute-start(bf16[2,8,512]{2,1,0:T(8,128)(2,1)S(1)} %pad_maximum_fusion.6), channel_id=1, source_target_pairs={{0,8},{8,16},{16,24},{24,0},{1,9},{9,17},{17,25},{25,1},{2,10},{10... | collective-permute-start | bytes 49160 | tf_op jit(solution)/shard_map/ppermute | solution.py:12
  37.4 4.7 %collective-permute-start.1 = (bf16[2,8,512]{2,1,0:T(8,128)(2,1)S(1)}, bf16[2,8,512]{2,1,0:T(8,128)(2,1)S(1)}, u32[]{:S(2)}, u32[]{:S(2)}) collective-permute-start(bf16[2,8,512]{2,1,0:T(8,128)(2,1)S(1)} %collective-permute-done), channel_id=1, source_target_pairs={{0,8},{8,16},{16,24},{24,0},{1,9},{9,17},{17,25},{25,1},{2,10},{10... | collective-permute-start | bytes 49160 | tf_op jit(solution)/shard_map/ppermute | solution.py:12
  56.3 4.7 %collective-permute-start.2 = (bf16[2,8,512]{2,1,0:T(8,128)(2,1)S(1)}, bf16[2,8,512]{2,1,0:T(8,128)(2,1)S(1)}, u32[]{:S(2)}, u32[]{:S(2)}) collective-permute-start(bf16[2,8,512]{2,1,0:T(8,128)(2,1)S(1)} %collective-permute-done.1), channel_id=1, source_target_pairs={{0,8},{8,16},{16,24},{24,0},{1,9},{9,17},{17,25},{25,1},{2,10},{10... | collective-permute-start | bytes 49160 | tf_op jit(solution)/shard_map/ppermute | solution.py:12
  75.5 1.4 %copy-start.1 = (bf16[256,512]{1,0:T(8,128)(2,1)S(1)}, bf16[256,512]{1,0:T(8,128)(2,1)}, u32[]{:S(2)}) copy-start(bf16[256,512]{1,0:T(8,128)(2,1)} %param.8) | copy-start | bytes 786436
  76.0 16.3 %slice-start = ((s8[4718592]{0:T(1024)(128)(4,1)}), s8[4194304]{0:T(1024)(128)(4,1)S(1)}, s32[]{:S(2)}) async-start(s8[4718592]{0:T(1024)(128)(4,1)} %bitcast.213), calls=%async_computation | async-start | bytes 8388608
  76.9 15.3 %slice-start.1 = ((s8[4718592]{0:T(1024)(128)(4,1)}), s8[524288]{0:T(1024)(128)(4,1)S(1)}, s32[]{:S(2)}) async-start(s8[4718592]{0:T(1024)(128)(4,1)} %bitcast.213), calls=%async_computation.1 | async-start | bytes 1048576
  77.6 7.2 %collective-permute-start.4 = (bf16[1,128,512]{2,1,0:T(8,128)(2,1)S(1)}, bf16[1,128,512]{2,1,0:T(8,128)(2,1)S(1)}, u32[]{:S(2)}, u32[]{:S(2)}) collective-permute-start(bf16[1,128,512]{2,1,0:T(8,128)(2,1)S(1)} %get-tuple-element.32), channel_id=1, source_target_pairs={{1,0},{2,1},{3,2},{4,3},{5,4},{6,5},{7,6},{8,7},{9,8},{10,9},{11,1... | collective-permute-start | bytes 393224 | tf_op jit(solution)/shard_map/ppermute | solution.py:23
  81.8 9.9 %collective-permute-start.3 = (bf16[1,128,512]{2,1,0:T(8,128)(2,1)S(1)}, bf16[1,128,512]{2,1,0:T(8,128)(2,1)S(1)}, u32[]{:S(2)}, u32[]{:S(2)}) collective-permute-start(bf16[1,128,512]{2,1,0:T(8,128)(2,1)S(1)} %get-tuple-element.33), channel_id=1, source_target_pairs={{0,1},{1,2},{2,3},{3,4},{4,5},{5,6},{6,7},{7,8},{8,9},{9,10},{10,1... | collective-permute-start | bytes 393224 | tf_op jit(solution)/shard_map/ppermute | solution.py:20
where the time goes:
time: 96.1 us; the launch traced here: 95.7 us
  blocking collectives  56.3 us (59%)
  waiting for transfers between devices  16 us (17%)
  matrix products  8.74 us (9%)
  starting transfers between devices  8.25 us (9%)
  local copies, waits for them, and re-layouts  3.22 us (3%)
  other arithmetic  2.77 us (3%)
    all_gather x4, blocking collectives, visit_shards(): collected = lax.all_gather(block, 'tile', axis=1, tiled=True)  56.3 us
    ppermute x3, waiting for transfers between devices, passed_along(): lax.ppermute(array, axis, [(i, (i + by) % peers) for i in range(peers)])  8.08 us
    ppermute x1, waiting for transfers between devices, with_halo(): lax.ppermute(lax.slice_in_dim(block, block.shape[dim] - width, None, axis...  6.96 us
    ppermute x1, starting transfers between devices, with_halo(): lax.ppermute(lax.slice_in_dim(block, 0, width, axis=dim), axis, backward)  4.25 us
    dot_general x9, matrix products, on_device(): jnp.dot(moved.reshape(q_dev, width), conv_weight[lat_off, lon_off], prefe...  3.39 us
    dot_general x4, matrix products, attend(): jnp.dot(mask_float, member.astype(jnp.float32).T, precision=lax.Precision...  3.22 us
    ppermute x3, starting transfers between devices, passed_along(): lax.ppermute(array, axis, [(i, (i + by) % peers) for i in range(peers)])  2.08 us
  transfers between devices with their start and end apart: 5, of which 4 were waited for; matrix products, arithmetic and copies ran while one was open for 8% of the time, Pallas kernels for 0%

commit v1 on v0

v1 whole, which is shorter than its diff:
```python
import functools
import math

import jax
import jax.numpy as jnp
from jax import lax
from jax.experimental import pallas as pl
from jax.experimental.pallas import tpu as pltpu
from jax.sharding import PartitionSpec as P

HEADS = 8
OBS_BLOCK = 128
AXES = ("blk", "tile")
PAIR = 2
MASK_ROWS = 16
NT = (((1,), (1,)), ((), ()))


def layer_kernel(
    tiles, lon, width, nblocks,
    edge_ref, mask_ref, valid_ref, low_ref, high_ref, queries_ref, grid_ref, kv_ref, out_weight_ref,
    conv_hbm, out_ref, conv_ref, mixed_ref, field_ref, conv_sem,
):
    head = width // HEADS
    pair = PAIR * head
    obs = nblocks * OBS_BLOCK
    scale = head ** (-0.5) * math.log2(math.e)
    copies = [
        pltpu.make_async_copy(conv_hbm.at[lat_off], conv_ref.at[lat_off], conv_sem.at[lat_off])
        for lat_off in range(3)
    ]
    for copy in copies:
        copy.start()

    key_lane = lax.broadcasted_iota(jnp.int32, (1, OBS_BLOCK), 1)

    def limited(allowed, block):
        live = key_lane < valid_ref[block]
        return jnp.where(jnp.logical_and(allowed, live), 0.0, -jnp.inf)

    def own_bias(tile):
        parts = [limited(mask_ref[tile, block] > 0, block) for block in range(nblocks)]
        return jnp.concatenate(parts, axis=1)

    def halo_bias(ref):
        row = ref[2 * lon : 2 * lon + MASK_ROWS, :].astype(jnp.float32)[:1]
        parts = [
            limited(jnp.broadcast_to(row[:, block : block + 1], (1, OBS_BLOCK)) > 0.5, block)
            for block in range(nblocks)
        ]
        return jnp.concatenate(parts, axis=1)

    biases = [halo_bias(low_ref)] + [own_bias(t) for t in range(tiles)] + [halo_bias(high_ref)]

    lane = lax.broadcasted_iota(jnp.int32, (obs, pair), 1)
    ones = [(lane // head == h).astype(jnp.bfloat16) for h in range(PAIR)]
    for group in range(HEADS // PAIR):
        cols = slice(group * pair, (group + 1) * pair)
        keys = kv_ref[:, :, group * pair : (group + 1) * pair].reshape(obs, pair)
        values = kv_ref[:, :, width + group * pair : width + (group + 1) * pair].reshape(obs, pair)
        key_parts = [keys * one for one in ones]
        value_parts = jnp.concatenate(
            [jnp.concatenate([values * one, one], axis=1) for one in ones], axis=0
        )
        rows = [low_ref[:lon, cols]]
        rows += [queries_ref[t * lon : (t + 1) * lon, cols] for t in range(tiles)]
        rows += [high_ref[:lon, cols]]
        query = jnp.concatenate(rows, axis=0)
        weights = []
        for part in key_parts:
            scores = lax.dot_general(query, part, NT, preferred_element_type=jnp.float32)
            pieces = []
            for t, bias in enumerate(biases):
                piece = scores[t * lon : (t + 1) * lon] * scale + bias
                top = jnp.max(piece, axis=1, keepdims=True)
                pieces.append(jnp.exp2(piece - top).astype(jnp.bfloat16))
            weights.append(jnp.concatenate(pieces, axis=0))
        both = jnp.dot(
            jnp.concatenate(weights, axis=1), value_parts, preferred_element_type=jnp.float32
        )
        mixed_ref[:, cols] = (both[:, :pair] / both[:, pair:]).astype(jnp.bfloat16)

    projected = jnp.dot(mixed_ref[...], out_weight_ref[...], preferred_element_type=jnp.float32)
    grid = jnp.concatenate(
        [low_ref[lon : 2 * lon, :], grid_ref[...], high_ref[lon : 2 * lon, :]], axis=0
    )
    hidden = (grid.astype(jnp.float32) + projected).astype(jnp.bfloat16)
    wide = hidden.astype(jnp.float32)
    normed = wide * lax.rsqrt(jnp.mean(wide * wide, axis=-1, keepdims=True) + 1e-06)
    last = (tiles + 1) * lon
    field_ref[lon:last] = normed[lon:last].astype(jnp.bfloat16)
    field_ref[:lon] = jnp.where(edge_ref[0] > 0, normed[:lon], 0.0).astype(jnp.bfloat16)
    field_ref[last:] = jnp.where(edge_ref[1] > 0, normed[last:], 0.0).astype(jnp.bfloat16)

    sums = [None, None, None]
    for lat_off in range(3):
        copies[lat_off].wait()
        moved = field_ref[lat_off * lon : (lat_off + tiles) * lon, :]
        for lon_off in range(3):
            term = jnp.dot(moved, conv_ref[lat_off, lon_off], preferred_element_type=jnp.float32)
            sums[lon_off] = term if sums[lon_off] is None else sums[lon_off] + term
    for t in range(tiles):
        here = slice(t * lon, (t + 1) * lon)
        out_ref[here, :] = (
            wide[(t + 1) * lon : (t + 2) * lon]
            + pltpu.roll(sums[0][here], 1, 0)
            + sums[1][here]
            + pltpu.roll(sums[2][here], lon - 1, 0)
        ).astype(jnp.bfloat16)


def on_device(
    grid_feat, queries, obs_keys, obs_values, block_mask, obs_valid, out_weight, conv_weight
):
    q_dev, width = queries.shape
    tiles, nblocks = block_mask.shape
    lon = q_dev // tiles
    devices = lax.axis_size(AXES)
    me = lax.axis_index(AXES)
    edge = jnp.stack([me > 0, me < devices - 1]).astype(jnp.int32)

    mask_tile = jnp.pad(block_mask.astype(jnp.bfloat16), ((0, 0), (0, width - nblocks)))

    def packed(tile):
        rows = slice(tile * lon, (tile + 1) * lon)
        mask = jnp.broadcast_to(mask_tile[tile : tile + 1], (MASK_ROWS, width))
        return jnp.concatenate([queries[rows], grid_feat[rows], mask], axis=0)

    forward = [(i, i + 1) for i in range(devices - 1)]
    backward = [(i + 1, i) for i in range(devices - 1)]
    low = lax.ppermute(packed(tiles - 1), AXES, forward)
    high = lax.ppermute(packed(0), AXES, backward)

    kv_local = jnp.concatenate([obs_keys, obs_values], axis=1)
    kv = lax.all_to_all(
        jnp.broadcast_to(kv_local[None], (devices,) + kv_local.shape), AXES, 0, 0
    )

    vmem = pl.BlockSpec(memory_space=pltpu.VMEM)
    smem = pl.BlockSpec(memory_space=pltpu.SMEM)
    flops = 2 * q_dev * width * (9 * width + 2 * width + 4 * nblocks * OBS_BLOCK)
    return pl.pallas_call(
        functools.partial(layer_kernel, tiles, lon, width, nblocks),
        out_shape=jax.ShapeDtypeStruct((q_dev, width), jnp.bfloat16),
        in_specs=[smem] * 3 + [vmem] * 6 + [pl.BlockSpec(memory_space=pl.ANY)],
        out_specs=vmem,
        scratch_shapes=[
            pltpu.VMEM(conv_weight.shape, jnp.bfloat16),
            pltpu.VMEM(((tiles + 2) * lon, width), jnp.bfloat16),
            pltpu.VMEM(((tiles + 2) * lon, width), jnp.bfloat16),
            pltpu.SemaphoreType.DMA((3,)),
        ],
        compiler_params=pltpu.CompilerParams(vmem_limit_bytes=48 * 2**20),
        cost_estimate=pl.CostEstimate(
            flops=flops, bytes_accessed=2 * conv_weight.size, transcendentals=0
        ),
        name="layer",
    )(edge, block_mask, obs_valid, low, high, queries, grid_feat, kv, out_weight, conv_weight)


def solution(mesh):
    in_specs = (
        P(AXES, None),
        P(AXES, None),
        P(AXES, None),
        P(AXES, None),
        P(AXES, None),
        P(),
        P(),
        P(),
    )
    return jax.shard_map(
        on_device, mesh=mesh, in_specs=in_specs, out_specs=P(AXES, None), check_vma=False
    )
```

time: 96.1 us -> 37.7 us (0.39)
  the two profiles are of different devices: /device:TPU:4 before, /device:TPU:9 now
where the time goes in v1:
time: 37.7 us; the launch traced here: 37.3 us
  waiting for transfers between devices  12.1 us (32%)
  starting transfers between devices  11.6 us (31%)
  local copies, waits for them, and re-layouts  6.29 us (17%)
  Pallas kernels  5.62 us (15%)
  other arithmetic  1.52 us (4%)
    ppermute x1, waiting for transfers between devices, on_device(): low = lax.ppermute(packed(tiles - 1), AXES, forward)  7.33 us
    all_to_all x1, starting transfers between devices, on_device(): lax.all_to_all(jnp.broadcast_to(kv_local[None], (devices,) + kv_local.sha...  6.36 us
    pallas_call x1, Pallas kernels, on_device(): pl.pallas_call(functools.partial(layer_kernel, tiles, lon, width, nblocks...  5.62 us
    ppermute x1, waiting for transfers between devices, on_device(): high = lax.ppermute(packed(0), AXES, backward)  4.82 us
    unnamed x10, local copies, waits for them, and re-layouts  4.27 us
    ppermute x1, starting transfers between devices, on_device(): low = lax.ppermute(packed(tiles - 1), AXES, forward)  3.34 us
    ppermute x1, starting transfers between devices, on_device(): high = lax.ppermute(packed(0), AXES, backward)  1.92 us
    slice x1, local copies, waits for them, and re-layouts, packed(): return jnp.concatenate([queries[rows], grid_feat[rows], mask], axis=0)  1.13 us
  transfers between devices with their start and end apart: 3, of which 2 were waited for; matrix products, arithmetic and copies ran while one was open for 5% of the time, Pallas kernels for 0%

profile of v1, /device:TPU:9, one launch (start us, length us, event | category | flops | bytes accessed | tf_op | source)
XLA Modules:
  0.0 37.3 jit_solution(15393580275986585934)
XLA Ops:
  0.0 0.7 %pad_maximum_fusion.2 = bf16[8,1024]{1,0:T(8,128)(2,1)S(1)} fusion(bf16[8,512]{1,0:T(8,128)(2,1)} %param.11, bf16[8,512]{1,0:T(8,128)(2,1)} %param.10), kind=kLoop, calls=%fused_computation.2 | loop fusion | flops 32768 | bytes 32768 | tf_op jit(solution)/shard_map/concatenate | solution.py:134
  0.7 0.8 %broadcast_in_dim.24 = bf16[32,8,1024]{2,1,0:T(8,128)(2,1)} broadcast(bf16[8,1024]{1,0:T(8,128)(2,1)S(1)} %pad_maximum_fusion.2), dimensions={1,2} | broadcast | bytes 540672 | tf_op jit(solution)/shard_map/broadcast_in_dim | solution.py:136
  1.6 6.4 %all-to-all-start = ((bf16[32,8,1024]{2,1,0:T(8,128)(2,1)}), bf16[32,8,1024]{2,1,0:T(8,128)(2,1)S(1)}, u32[]{:S(2)}, u32[]{:S(2)}) async-start(bf16[32,8,1024]{2,1,0:T(8,128)(2,1)} %broadcast_in_dim.24), calls=%async_computation | async-start | bytes 1048576 | tf_op jit(solution)/shard_map/all_to_all | solution.py:135
  7.9 0.7 %convert_element_type.9 = bf16[2,2]{1,0:T(2,128)(2,1)S(1)} convert(s32[2,2]{1,0:T(2,128)} %mask_ref.1) | non-fusion elementwise | flops 4 | bytes 24 | tf_op jit(solution)/shard_map/convert_element_type | solution.py:122
  8.6 1.1 %fusion = (bf16[128,512]{1,0:T(8,128)(2,1)S(1)}, bf16[128,512]{1,0:T(8,128)(2,1)S(1)}, bf16[128,512]{1,0:T(8,128)(2,1)S(1)}, bf16[128,512]{1,0:T(8,128)(2,1)S(1)}) fusion(bf16[256,512]{1,0:T(8,128)(2,1)} %queries_ref.1, bf16[256,512]{1,0:T(8,128)(2,1)} %grid_ref.1), kind=kLoop, calls=%fused_computation.6 | loop fusion | bytes 1048576 | tf_op jit(solution)/shard_map/slice | solution.py:127
  9.8 3.3 %collective-permute-start = (bf16[272,512]{1,0:T(8,128)(2,1)S(1)}, bf16[272,512]{1,0:T(8,128)(2,1)S(1)}, u32[]{:S(2)}, u32[]{:S(2)}) collective-permute-start(bf16[272,512]{1,0:T(8,128)(2,1)S(1)} %pad_maximum_fusion), channel_id=1, source_target_pairs={{0,1},{1,2},{2,3},{3,4},{4,5},{5,6},{6,7},{7,8},{8,9},{9,10},{10,1... | collective-permute-start | bytes 835592 | tf_op jit(solution)/shard_map/ppermute | solution.py:131
  13.2 1.9 %collective-permute-start.1 = (bf16[272,512]{1,0:T(8,128)(2,1)S(1)}, bf16[272,512]{1,0:T(8,128)(2,1)S(1)}, u32[]{:S(2)}, u32[]{:S(2)}) collective-permute-start(bf16[272,512]{1,0:T(8,128)(2,1)S(1)} %pad_maximum_fusion.1), channel_id=1, source_target_pairs={{1,0},{2,1},{3,2},{4,3},{5,4},{6,5},{7,6},{8,7},{9,8},{10,9},{11,1... | collective-permute-start | bytes 835592 | tf_op jit(solution)/shard_map/ppermute | solution.py:132
  15.2 0.1 add_convert_fusion.edge_ref
  15.2 7.3 %collective-permute-done.low_ref = bf16[272,512]{1,0:T(8,128)(2,1)S(1)} collective-permute-done((bf16[272,512]{1,0:T(8,128)(2,1)S(1)}, bf16[272,512]{1,0:T(8,128)(2,1)S(1)}, u32[]{:S(2)}, u32[]{:S(2)}) %collective-permute-start) | collective-permute-done | bytes 278560 | tf_op jit(solution)/shard_map/ppermute | solution.py:131
  22.6 4.8 %collective-permute-done.1.high_ref = bf16[272,512]{1,0:T(8,128)(2,1)S(1)} collective-permute-done((bf16[272,512]{1,0:T(8,128)(2,1)S(1)}, bf16[272,512]{1,0:T(8,128)(2,1)S(1)}, u32[]{:S(2)}, u32[]{:S(2)}) %collective-permute-start.1) | collective-permute-done | bytes 278560 | tf_op jit(solution)/shard_map/ppermute | solution.py:132
  27.4 0.0 all-to-all-done.kv_ref
  27.4 0.0 copy-start
  27.4 0.9 %copy-done = bf16[256,512]{1,0:T(8,128)(2,1)S(1)} copy-done((bf16[256,512]{1,0:T(8,128)(2,1)S(1)}, bf16[256,512]{1,0:T(8,128)(2,1)}, u32[]{:S(2)}) %copy-start) | copy-done | bytes 262168
  28.3 0.0 copy-start.1
  28.3 0.9 %copy-done.1 = bf16[256,512]{1,0:T(8,128)(2,1)S(1)} copy-done((bf16[256,512]{1,0:T(8,128)(2,1)S(1)}, bf16[256,512]{1,0:T(8,128)(2,1)}, u32[]{:S(2)}) %copy-start.1) | copy-done | bytes 262168
  29.3 0.0 copy-start.2
  29.3 1.0 %copy-done.2 = bf16[512,512]{1,0:T(8,128)(2,1)S(1)} copy-done((bf16[512,512]{1,0:T(8,128)(2,1)S(1)}, bf16[512,512]{1,0:T(8,128)(2,1)}, u32[]{:S(2)}) %copy-start.2) | copy-done | bytes 524312
  30.3 0.0 copy-start.3
  30.3 0.7 %copy-done.3 = s32[2,2]{1,0:T(2,128)S(1)} copy-done((s32[2,2]{1,0:T(2,128)S(1)}, s32[2,2]{1,0:T(2,128)}, u32[]{:S(2)}) %copy-start.3) | copy-done | bytes 40
  31.0 0.0 copy-start.4
  31.0 0.7 %copy-done.4 = s32[2]{0:T(128)S(1)} copy-done((s32[2]{0:T(128)S(1)}, s32[2]{0:T(128)}, u32[]{:S(2)}) %copy-start.4) | copy-done | bytes 32
  31.7 5.6 %layer.1 = bf16[256,512]{1,0:T(8,128)(2,1)} custom-call(s32[2]{0:T(128)S(1)} %add_convert_fusion.edge_ref, s32[2,2]{1,0:T(2,128)S(1)} %copy-done.3, s32[2]{0:T(128)S(1)} %copy-done.4, bf16[272,512]{1,0:T(8,128)(2,1)S(1)} %collective-permute-done.low_ref, bf16[272,512]{1,0:T(8,128)(2,1)S(1)} %collective-permute-done.1.high_ref, bf16[256,512]{1,0:T(8,128)(2,1)S(1)} %copy-done, ...), custom_call_target="tpu_custom_call" | custom-call | flops 1744830464 | bytes 4718592 | tf_op jit(solution)/shard_map/layer/pallas_call | solution.py:142
  (5 shorter events, 0.1 us)
Async XLA Ops:
  1.6 25.8 %all-to-all-start = ((bf16[32,8,1024]{2,1,0:T(8,128)(2,1)}), bf16[32,8,1024]{2,1,0:T(8,128)(2,1)S(1)}, u32[]{:S(2)}, u32[]{:S(2)}) async-start(bf16[32,8,1024]{2,1,0:T(8,128)(2,1)} %broadcast_in_dim.24), calls=%async_computation | async-start | bytes 1048576 | tf_op jit(solution)/shard_map/all_to_all | solution.py:135
  9.8 12.7 %collective-permute-start = (bf16[272,512]{1,0:T(8,128)(2,1)S(1)}, bf16[272,512]{1,0:T(8,128)(2,1)S(1)}, u32[]{:S(2)}, u32[]{:S(2)}) collective-permute-start(bf16[272,512]{1,0:T(8,128)(2,1)S(1)} %pad_maximum_fusion), channel_id=1, source_target_pairs={{0,1},{1,2},{2,3},{3,4},{4,5},{5,6},{6,7},{7,8},{8,9},{9,10},{10,1... | collective-permute-start | bytes 835592 | tf_op jit(solution)/shard_map/ppermute | solution.py:131
  13.2 14.2 %collective-permute-start.1 = (bf16[272,512]{1,0:T(8,128)(2,1)S(1)}, bf16[272,512]{1,0:T(8,128)(2,1)S(1)}, u32[]{:S(2)}, u32[]{:S(2)}) collective-permute-start(bf16[272,512]{1,0:T(8,128)(2,1)S(1)} %pad_maximum_fusion.1), channel_id=1, source_target_pairs={{1,0},{2,1},{3,2},{4,3},{5,4},{6,5},{7,6},{8,7},{9,8},{10,9},{11,1... | collective-permute-start | bytes 835592 | tf_op jit(solution)/shard_map/ppermute | solution.py:132
  27.4 1.0 %copy-start = (bf16[256,512]{1,0:T(8,128)(2,1)S(1)}, bf16[256,512]{1,0:T(8,128)(2,1)}, u32[]{:S(2)}) copy-start(bf16[256,512]{1,0:T(8,128)(2,1)} %queries_ref.1) | copy-start | bytes 786436
  28.3 0.9 %copy-start.1 = (bf16[256,512]{1,0:T(8,128)(2,1)S(1)}, bf16[256,512]{1,0:T(8,128)(2,1)}, u32[]{:S(2)}) copy-start(bf16[256,512]{1,0:T(8,128)(2,1)} %grid_ref.1) | copy-start | bytes 786436
  29.3 1.0 %copy-start.2 = (bf16[512,512]{1,0:T(8,128)(2,1)S(1)}, bf16[512,512]{1,0:T(8,128)(2,1)}, u32[]{:S(2)}) copy-start(bf16[512,512]{1,0:T(8,128)(2,1)} %out_weight_ref.1) | copy-start | bytes 1572868
  30.3 0.7 %copy-start.3 = (s32[2,2]{1,0:T(2,128)S(1)}, s32[2,2]{1,0:T(2,128)}, u32[]{:S(2)}) copy-start(s32[2,2]{1,0:T(2,128)} %mask_ref.1) | copy-start | bytes 52
  31.0 0.7 %copy-start.4 = (s32[2]{0:T(128)S(1)}, s32[2]{0:T(128)}, u32[]{:S(2)}) copy-start(s32[2]{0:T(128)} %valid_ref.1) | copy-start | bytes 28
